TPU v7x, 512 devices: a whole 4x4x16 slice. The times are simulated.
512 devices in a mesh: det: 2 (over core), bank: 128 (over z, x_hi, y), seg: 2 (over x_lo).
Axes of the slice: x: 4 (x_hi: 2, x_lo: 2; x = x_hi * 2 + x_lo), y: 4, z: 16, core: 2. Of those that a mesh axis runs over, the one named last changes fastest.
Arguments:
- strain: bfloat16 [2, 2, 2048], P('det', 'seg', 'bank'), may hold values from -6 to 6
- basis_filters: bfloat16 [128, 512, 640], P('bank', None, 'seg'), may hold values from -0.25 to 0.25
- template_mix: bfloat16 [128, 640, 2, 512], P('bank', None, None, 'seg'), may hold values from -0.25 to 0.25
- basis_counts: int32 [128], P('bank'), may hold values from 200 to 600, as said below
- window_bins: int32 [65536], P(('bank', 'seg')), may hold values from 0 to 2
- time_slides: int32 [2], replicated, may hold values from 0 to 31
Outputs:
- coincident_snr: float32 [65536], P(('bank', 'seg'))
Inputs may be any that keep to these rules, and one draw needn't show every extreme that they name: `basis_counts`: slots of a sub-bank from its count up to 640 are padding.
All inputs are finite; a program needn't handle non-finite values.
Results may differ from a plain program's by a relative error of at most 0.00067.
Values may be sent and summed in bfloat16 or wider, within the bound.
No kernel may reach another device: no remote copies, remote signals or barrier semaphores. Data moves between devices by JAX's collectives and lax.ppermute only.
A program may use at most 64 MiB of HBM per device.

v0:
```python
import jax
import jax.numpy as jnp
from jax import lax
from jax.experimental import pallas as pl
from jax.experimental.pallas import tpu as pltpu
from jax.sharding import Mesh, PartitionSpec as P

BIN = 128
WMAX = 2
LANES = 128
PLANE = ("det", "xh", "y", "seg")
BANK = ("z", "xh", "y")


def filters_kernel(count_ref, own_ref, other_ref, mix_ref, out_ref):
    seg = lax.axis_index("seg")
    det = lax.axis_index("det")
    half = own_ref.shape[0]
    width = out_ref.shape[1] // 2
    count = count_ref[0]
    columns = pl.ds(pl.multiple_of(det * width, LANES), width)
    for quad in range(2):
        total = None
        for place, filters in ((seg, own_ref), (1 - seg, other_ref)):
            first = pl.multiple_of(place * half, 64)
            coefs = mix_ref[quad, pl.ds(first, half), columns]
            slot = first + lax.broadcasted_iota(jnp.int32, coefs.shape, 0)
            coefs = jnp.where(slot < count, coefs.astype(jnp.float32), 0.0).astype(jnp.bfloat16)
            part = lax.dot_general(
                filters[...], coefs, (((0,), (0,)), ((), ())), preferred_element_type=jnp.float32
            )
            total = part if total is None else total + part
        out_ref[:, quad * width : (quad + 1) * width] = total.astype(jnp.bfloat16)


def peaks_kernel(slides_ref, pieces_ref, filt_ref, limits_ref, out_ref, hankel, power):
    n_pieces, n_z, _ = pieces_ref.shape
    fine = n_pieces // 4
    step = LANES // fine
    bins = 2 * n_z
    taps = filt_ref.shape[0]
    spans = taps // LANES
    width = filt_ref.shape[1] // 2
    row = lax.broadcasted_iota(jnp.int32, (BIN, LANES), 0)
    lane = lax.broadcasted_iota(jnp.int32, (BIN, LANES), 1)
    early = lane <= row
    filt = filt_ref[...]
    group = 8
    for det in range(2):
        rows = []
        for seg in range(2):
            total = None
            for piece in range(fine):
                samples = pieces_ref[(det * fine + piece) * 2 + seg].astype(jnp.float32)
                if piece:
                    samples = pltpu.roll(samples, piece * step, 1)
                total = samples if total is None else total + samples
            rows.append(total)
        series = jnp.concatenate(rows, axis=0)

        def turned(c):
            return pltpu.roll(
                jnp.broadcast_to(series[c : c + 1], (BIN, LANES)), 1, 1, stride=1, stride_axis=0
            )

        here = turned(0)
        for c in range(bins + spans - 1):
            after = turned(c + 1) if c + 1 < bins else jnp.zeros((BIN, LANES), jnp.float32)
            tile = jnp.where(early, here, after).astype(jnp.bfloat16)
            here = after
            for span in range(spans):
                if 0 <= c - span < bins:
                    hankel[pl.ds((c - span) * BIN, BIN), span * LANES : (span + 1) * LANES] = tile
        for first in range(0, bins, group):
            snr = jnp.dot(
                hankel[pl.ds(first * BIN, group * BIN), :], filt, preferred_element_type=jnp.float32
            )
            real, imag = snr[:, :width], snr[:, width:]
            squared = (real * real + imag * imag).reshape(group, BIN, width)
            peak = jnp.max(squared, axis=1)
            for copy in range(3):
                power[det, pl.ds(copy * bins + first, group), :] = peak

    which = lax.axis_index("det")
    limits = jnp.where(which == 0, limits_ref[0:1], limits_ref[1:2])
    first_det = power[0, pl.ds(bins + slides_ref[0], bins), :]
    best = power[1, pl.ds(bins + slides_ref[1], bins), :]
    for offset in range(1, WMAX + 1):
        for direction in (1, -1):
            moved = power[1, pl.ds(bins + slides_ref[1] + direction * offset, bins), :]
            best = jnp.maximum(best, jnp.where(limits >= offset, moved, 0.0))
    out_ref[...] = jnp.sqrt(jnp.max(first_det + best, axis=0, keepdims=True))


def shards(strain, basis_filters, template_mix, basis_counts, window_bins, time_slides):
    taps = basis_filters.shape[1]
    width = template_mix.shape[3] // 2
    n_z = lax.axis_size("z")
    n_plane = 1
    for axis in PLANE:
        n_plane *= lax.axis_size(axis)
    bins = lax.axis_size("seg") * n_z

    vmem = pl.BlockSpec(memory_space=pltpu.VMEM)
    smem = pl.BlockSpec(memory_space=pltpu.SMEM)

    own = jnp.transpose(basis_filters[0])
    other = lax.ppermute(own, "seg", [(0, 1), (1, 0)])

    piece = jnp.pad(strain[0, 0].astype(jnp.float32), (0, LANES - strain.shape[2]))
    along = lax.all_to_all(
        jnp.broadcast_to(piece[None, None], (n_z, 1, LANES)), "z", 0, 0, tiled=True
    )
    along = along.reshape(n_z, LANES).astype(jnp.bfloat16)
    pieces = lax.all_to_all(
        jnp.broadcast_to(along[None], (n_plane, n_z, LANES)), PLANE, 0, 0, tiled=True
    )

    mix = jnp.transpose(template_mix[0], (1, 0, 2))
    filt = pl.pallas_call(
        filters_kernel,
        out_shape=jax.ShapeDtypeStruct((taps, 2 * width), jnp.bfloat16),
        in_specs=[smem, vmem, vmem, vmem],
        out_specs=vmem,
        compiler_params=pltpu.CompilerParams(vmem_limit_bytes=24 << 20),
        cost_estimate=pl.CostEstimate(
            flops=4 * taps * width * mix.shape[1], bytes_accessed=2 << 20, transcendentals=0
        ),
    )(basis_counts, own, other, mix)
    mine = pl.pallas_call(
        peaks_kernel,
        out_shape=jax.ShapeDtypeStruct((1, width), jnp.float32),
        in_specs=[smem, vmem, vmem, vmem],
        out_specs=vmem,
        scratch_shapes=[
            pltpu.VMEM((bins * BIN, taps), jnp.bfloat16),
            pltpu.VMEM((2, 3 * bins, width), jnp.float32),
        ],
        compiler_params=pltpu.CompilerParams(vmem_limit_bytes=32 << 20),
    )(time_slides, pieces, filt, window_bins.reshape(2, width))
    return lax.all_gather(mine, "det", axis=0, tiled=True).reshape(2 * width)


def solution(mesh):
    n_det, n_bank, n_seg = mesh.devices.shape
    fine = Mesh(mesh.devices.reshape(n_det, n_bank // 8, 2, 4, n_seg), ("det", "z", "xh", "y", "seg"))
    placed = (
        P("det", "seg", BANK),
        P(BANK, None, "seg"),
        P(BANK, None, None, "seg"),
        P(BANK),
        P((*BANK, "seg")),
        P(),
    )
    return jax.shard_map(
        shards, mesh=fine, in_specs=placed, out_specs=P((*BANK, "seg")), check_vma=False
    )
```

profile of v0, /device:TPU:1, one launch (start us, length us, event | category | flops | bytes accessed | tf_op | source)
XLA Modules:
  0.0 51.8 jit_solution(8050425483900175748)
XLA Ops:
  0.0 0.0 copy-start.3
  0.0 0.7 %copy-done.3 = bf16[1,1,16]{2,1,0:T(2,128)(2,1)S(1)} copy-done((bf16[1,1,16]{2,1,0:T(2,128)(2,1)S(1)}, bf16[1,1,16]{2,1,0:T(2,128)(2,1)}, u32[]{:S(2)}) %copy-start.3) | copy-done | bytes 56
  0.7 0.6 %broadcast_in_dim.4 = f32[16,1,128]{2,1,0:T(1,128)} broadcast(f32[128]{0:T(128)S(1)} %pad_convert_fusion), dimensions={2} | broadcast | bytes 8704 | tf_op jit(solution)/shard_map/broadcast_in_dim | solution.py:112
  1.3 15.7 %all-to-all-start = ((f32[16,1,128]{2,1,0:T(1,128)}), f32[16,1,128]{2,1,0:T(1,128)S(1)}, u32[]{:S(2)}, u32[]{:S(2)}) async-start(f32[16,1,128]{2,1,0:T(1,128)} %broadcast_in_dim.4), calls=%async_computation | async-start | bytes 16384 | tf_op jit(solution)/shard_map/all_to_all | solution.py:111
  17.0 3.1 %collective-permute-start = (bf16[320,512]{1,0:T(8,128)(2,1)}, bf16[320,512]{1,0:T(8,128)(2,1)S(1)}, u32[]{:S(2)}, u32[]{:S(2)}) collective-permute-start(bf16[320,512]{1,0:T(8,128)(2,1)} %bitcast.16), channel_id=1, source_target_pairs={{0,1},{1,0},{2,3},{3,2},{4,5},{5,4},{6,7},{7,6},{8,9},{9,8},{10,11... | collective-permute-start | bytes 983048 | tf_op jit(solution)/shard_map/ppermute | solution.py:108
  20.1 8.2 %all-to-all-done = f32[16,1,128]{2,1,0:T(1,128)S(1)} async-done(((f32[16,1,128]{2,1,0:T(1,128)}), f32[16,1,128]{2,1,0:T(1,128)S(1)}, u32[]{:S(2)}, u32[]{:S(2)}) %all-to-all-start) | async-done | bytes 8224 | tf_op jit(solution)/shard_map/all_to_all | solution.py:111
  28.3 0.7 %broadcast_in_dim.5 = bf16[32,16,128]{2,1,0:T(8,128)(2,1)} broadcast(bf16[16,128]{1,0:T(8,128)(2,1)S(1)} %convert_bitcast_fusion), dimensions={1,2} | broadcast | bytes 135168 | tf_op jit(solution)/shard_map/broadcast_in_dim | solution.py:116
  29.0 9.1 %all-to-all-start.1 = ((bf16[32,16,128]{2,1,0:T(8,128)(2,1)}), bf16[32,16,128]{2,1,0:T(8,128)(2,1)S(1)}, u32[]{:S(2)}, u32[]{:S(2)}) async-start(bf16[32,16,128]{2,1,0:T(8,128)(2,1)} %broadcast_in_dim.5), calls=%async_computation.1 | async-start | bytes 262144 | tf_op jit(solution)/shard_map/all_to_all | solution.py:115
  38.1 0.0 copy-start
  38.1 1.2 %copy.12 = bf16[1,640,2,256]{3,1,2,0:T(8,128)(2,1)S(1)} copy(bf16[1,640,2,256]{3,2,1,0:T(2,128)(2,1)} %param.8) | data formatting | bytes 1310720 | tf_op args[2]
  40.0 0.0 collective-permute-done.other_ref
  40.0 0.0 copy-done
  40.0 0.6 %shard_map.64.filt_ref = bf16[512,256]{1,0:T(8,128)(2,1)S(1)} custom-call(s32[1]{0:T(128)S(6)} %copy.14.count_ref, bf16[320,512]{1,0:T(8,128)(2,1)S(1)} %bitcast.17, bf16[320,512]{1,0:T(8,128)(2,1)S(1)} %collective-permute-done.other_ref, bf16[2,640,256]{2,1,0:T(8,128)(2,1)S(1)} %bitcast.15), custom_call_target="tpu_custom_call" | custom-call | flops 167772160 | bytes 2097152 | tf_op jit(solution)/shard_map/pallas_call | solution.py:120
  40.7 0.0 copy-start.1
  40.7 0.0 copy-start.2
  40.7 5.1 %all-to-all-done.1.pieces_ref = bf16[32,16,128]{2,1,0:T(8,128)(2,1)S(1)} async-done(((bf16[32,16,128]{2,1,0:T(8,128)(2,1)}), bf16[32,16,128]{2,1,0:T(8,128)(2,1)S(1)}, u32[]{:S(2)}, u32[]{:S(2)}) %all-to-all-start.1) | async-done | bytes 131104 | tf_op jit(solution)/shard_map/all_to_all | solution.py:115
  45.7 0.0 copy-done.1
  45.7 0.0 copy-done.2
  45.7 3.5 %shard_map.65 = f32[1,128]{1,0:T(1,128)S(1)} custom-call(s32[2]{0:T(128)S(1)} %copy-done.2, bf16[32,16,128]{2,1,0:T(8,128)(2,1)S(1)} %all-to-all-done.1.pieces_ref, bf16[512,256]{1,0:T(8,128)(2,1)S(1)} %shard_map.64.filt_ref, s32[2,128]{1,0:T(2,128)S(1)} %bitcast.18), custom_call_target="tpu_custom_call" | custom-call | tf_op jit(solution)/shard_map/pallas_call | solution.py:130
  49.2 2.0 %all-gather = f32[2,1,128]{2,1,0:T(1,128)S(1)} all-gather(f32[1,1,128]{2,1,0:T(1,128)S(1)} %bitcast.19), channel_id=1, replica_groups=mesh['det'=2,'z'=16,'xh'=2,'y'=4,'seg'=2] {'det'}, dimensions={0}, use_global_device_ids=true | all-gather | bytes 1536 | tf_op jit(solution)/shard_map/all_gather | solution.py:141
  51.2 0.6 %copy.15 = f32[256]{0:T(256)} copy(f32[256]{0:T(256)S(1)} %bitcast.21) | data formatting | bytes 2048
  (2 shorter events, 0.0 us)
Async XLA Ops:
  0.0 0.7 %copy-start.3 = (bf16[1,1,16]{2,1,0:T(2,128)(2,1)S(1)}, bf16[1,1,16]{2,1,0:T(2,128)(2,1)}, u32[]{:S(2)}) copy-start(bf16[1,1,16]{2,1,0:T(2,128)(2,1)} %param.6) | copy-start | bytes 100
  1.3 27.1 %all-to-all-start = ((f32[16,1,128]{2,1,0:T(1,128)}), f32[16,1,128]{2,1,0:T(1,128)S(1)}, u32[]{:S(2)}, u32[]{:S(2)}) async-start(f32[16,1,128]{2,1,0:T(1,128)} %broadcast_in_dim.4), calls=%async_computation | async-start | bytes 16384 | tf_op jit(solution)/shard_map/all_to_all | solution.py:111
  17.0 23.0 %collective-permute-start = (bf16[320,512]{1,0:T(8,128)(2,1)}, bf16[320,512]{1,0:T(8,128)(2,1)S(1)}, u32[]{:S(2)}, u32[]{:S(2)}) collective-permute-start(bf16[320,512]{1,0:T(8,128)(2,1)} %bitcast.16), channel_id=1, source_target_pairs={{0,1},{1,0},{2,3},{3,2},{4,5},{5,4},{6,7},{7,6},{8,9},{9,8},{10,11... | collective-permute-start | bytes 983048 | tf_op jit(solution)/shard_map/ppermute | solution.py:108
  29.0 16.7 %all-to-all-start.1 = ((bf16[32,16,128]{2,1,0:T(8,128)(2,1)}), bf16[32,16,128]{2,1,0:T(8,128)(2,1)S(1)}, u32[]{:S(2)}, u32[]{:S(2)}) async-start(bf16[32,16,128]{2,1,0:T(8,128)(2,1)} %broadcast_in_dim.5), calls=%async_computation.1 | async-start | bytes 262144 | tf_op jit(solution)/shard_map/all_to_all | solution.py:115
  38.1 1.9 %copy-start = (bf16[1,512,320]{1,2,0:T(8,128)(2,1)S(1)}, bf16[1,512,320]{1,2,0:T(8,128)(2,1)}, u32[]{:S(2)}) copy-start(bf16[1,512,320]{1,2,0:T(8,128)(2,1)} %param.7) | copy-start | bytes 983044
  40.7 5.1 %copy-start.1 = (s32[256]{0:T(256)S(1)}, s32[256]{0:T(256)}, u32[]{:S(2)}) copy-start(s32[256]{0:T(256)} %param.10) | copy-start | bytes 3076
  40.7 5.1 %copy-start.2 = (s32[2]{0:T(128)S(1)}, s32[2]{0:T(128)}, u32[]{:S(2)}) copy-start(s32[2]{0:T(128)} %slides_ref.1) | copy-start | bytes 28
where the time goes:
time: 52 us; the launch traced here: 51.8 us
  starting transfers between devices  28 us (54%)
  waiting for transfers between devices  13.2 us (25%)
  Pallas kernels  4.08 us (8%)
  local copies, waits for them, and re-layouts  3.73 us (7%)
  blocking collectives  2 us (4%)
  between operations  0.73 us (1%)
    all_to_all x1, starting transfers between devices, shards(): lax.all_to_all(jnp.broadcast_to(piece[None, None], (n_z, 1, LANES)), 'z',...  15.7 us
    all_to_all x1, starting transfers between devices, shards(): lax.all_to_all(jnp.broadcast_to(along[None], (n_plane, n_z, LANES)), PLAN...  9.12 us
    all_to_all x1, waiting for transfers between devices, shards(): lax.all_to_all(jnp.broadcast_to(piece[None, None], (n_z, 1, LANES)), 'z',...  8.17 us
    all_to_all x1, waiting for transfers between devices, shards(): lax.all_to_all(jnp.broadcast_to(along[None], (n_plane, n_z, LANES)), PLAN...  5.05 us
    pallas_call x1, Pallas kernels, shards(): pl.pallas_call(peaks_kernel, out_shape=jax.ShapeDtypeStruct((1, width), j...  3.45 us
    ppermute x1, starting transfers between devices, shards(): other = lax.ppermute(own, 'seg', [(0, 1), (1, 0)])  3.12 us
    unnamed x10, local copies, waits for them, and re-layouts  2.46 us
    all_gather x1, blocking collectives, shards(): return lax.all_gather(mine, 'det', axis=0, tiled=True).reshape(2 * width)  2 us
  transfers between devices with their start and end apart: 3, of which 2 were waited for; matrix products, arithmetic and copies ran while one was open for 4% of the time, Pallas kernels for 1%

commit v1 on v0

v1 whole, which is shorter than its diff:
```python
import jax
import jax.numpy as jnp
from jax import lax
from jax.experimental import pallas as pl
from jax.experimental.pallas import tpu as pltpu
from jax.sharding import Mesh, PartitionSpec as P

BIN = 128
WMAX = 2
FIRST_Z = 11
LANES = 128
CHIPS = ("xh", "y", "seg", "z")
BANK = ("z", "xh", "y")


def filters_kernel(count_ref, own_ref, other_ref, mix_ref, out_ref):
    seg = lax.axis_index("seg")
    half = own_ref.shape[0]
    width = mix_ref.shape[2]
    count = count_ref[0]
    for quad in range(2):
        total = None
        for place, filters in ((seg, own_ref), (1 - seg, other_ref)):
            first = pl.multiple_of(place * half, 64)
            coefs = mix_ref[quad, pl.ds(first, half), :]
            slot = first + lax.broadcasted_iota(jnp.int32, coefs.shape, 0)
            coefs = jnp.where(slot < count, coefs.astype(jnp.float32), 0.0).astype(jnp.bfloat16)
            part = lax.dot_general(
                filters[...], coefs, (((0,), (0,)), ((), ())), preferred_element_type=jnp.float32
            )
            total = part if total is None else total + part
        out_ref[:, quad * width : (quad + 1) * width] = total.astype(jnp.bfloat16)


def peaks_kernel(slides_ref, pieces_ref, filt_ref, limits_ref, out_ref, hankel, power):
    bins, width = out_ref.shape
    n_z = bins // 2
    fine = pieces_ref.shape[0] // bins
    step = LANES // fine
    taps = filt_ref.shape[0]
    spans = taps // LANES
    group = 4
    row = lax.broadcasted_iota(jnp.int32, (BIN, LANES), 0)
    lane = lax.broadcasted_iota(jnp.int32, (BIN, LANES), 1)
    early = lane <= row
    filt = filt_ref[...]
    series = None
    for piece in range(fine):
        rows = []
        for first in (piece * bins, piece * bins + n_z):
            mark = first + n_z - FIRST_Z
            rows += [pieces_ref[mark : first + n_z, :], pieces_ref[first:mark, :]]
        samples = jnp.concatenate(rows, axis=0)
        if piece:
            samples = pltpu.roll(samples, piece * step, 1)
        series = samples if series is None else series + samples

    def turned(c):
        return pltpu.roll(
            jnp.broadcast_to(series[c : c + 1], (BIN, LANES)), 1, 1, stride=1, stride_axis=0
        )

    here = turned(0)
    for c in range(bins + spans - 1):
        after = turned(c + 1) if c + 1 < bins else jnp.zeros((BIN, LANES), jnp.float32)
        tile = jnp.where(early, here, after).astype(jnp.bfloat16)
        here = after
        for span in range(spans):
            if 0 <= c - span < bins:
                hankel[pl.ds((c - span) * BIN, BIN), span * LANES : (span + 1) * LANES] = tile
    for first in range(0, bins, group):
        snr = jnp.dot(
            hankel[pl.ds(first * BIN, group * BIN), :], filt, preferred_element_type=jnp.float32
        )
        real, imag = snr[:, :width], snr[:, width:]
        squared = (real * real + imag * imag).reshape(group, BIN, width)
        peak = jnp.max(squared, axis=1)
        power[pl.ds(first, group), :] = peak

    det = lax.axis_index("det")
    limits = jnp.where(det == 0, 0, limits_ref[...])
    shifted = pltpu.roll(power[...], lax.rem(bins - slides_ref[det], bins), 0)
    best = shifted
    for offset in range(1, WMAX + 1):
        for turn in (offset, bins - offset):
            moved = pltpu.roll(shifted, turn, 0)
            best = jnp.maximum(best, jnp.where(limits >= offset, moved, 0.0))
    out_ref[...] = best


def shards(strain, basis_filters, template_mix, basis_counts, window_bins, time_slides):
    taps = basis_filters.shape[1]
    width = template_mix.shape[3]
    n_chips = 1
    for axis in CHIPS:
        n_chips *= lax.axis_size(axis)
    bins = lax.axis_size("seg") * lax.axis_size("z")

    vmem = pl.BlockSpec(memory_space=pltpu.VMEM)
    smem = pl.BlockSpec(memory_space=pltpu.SMEM)

    own = jnp.transpose(basis_filters[0])
    other = lax.ppermute(own, "seg", [(0, 1), (1, 0)])

    piece = jnp.pad(strain[0, 0].astype(jnp.float32), (0, LANES - strain.shape[2]))
    n_z = lax.axis_size("z")
    order = [c - c % n_z + (c + FIRST_Z) % n_z for c in range(n_chips)]
    pieces = lax.all_to_all(
        jnp.broadcast_to(piece[None, None], (n_chips, 1, LANES)),
        CHIPS,
        0,
        0,
        axis_index_groups=[order],
        tiled=True,
    ).reshape(n_chips, LANES)

    mix = jnp.transpose(template_mix[0], (1, 0, 2))
    filt = pl.pallas_call(
        filters_kernel,
        out_shape=jax.ShapeDtypeStruct((taps, 2 * width), jnp.bfloat16),
        in_specs=[smem, vmem, vmem, vmem],
        out_specs=vmem,
        compiler_params=pltpu.CompilerParams(vmem_limit_bytes=24 << 20),
        cost_estimate=pl.CostEstimate(
            flops=1 * 4 * taps * width * mix.shape[1], bytes_accessed=2 << 20, transcendentals=0
        ),
    )(basis_counts, own, other, mix)
    mine = pl.pallas_call(
        peaks_kernel,
        out_shape=jax.ShapeDtypeStruct((bins, width), jnp.float32),
        in_specs=[smem, vmem, vmem, vmem],
        out_specs=vmem,
        scratch_shapes=[
            pltpu.VMEM((bins * BIN, taps), jnp.bfloat16),
            pltpu.VMEM((bins, width), jnp.float32),
        ],
        compiler_params=pltpu.CompilerParams(vmem_limit_bytes=32 << 20),
    )(time_slides, pieces, filt, window_bins.reshape(1, width))
    both = lax.all_gather(mine, "det", axis=0, tiled=False)
    return jnp.sqrt(jnp.max(both[0] + both[1], axis=0))


def solution(mesh):
    n_det, n_bank, n_seg = mesh.devices.shape
    fine = Mesh(mesh.devices.reshape(n_det, n_bank // 8, 2, 4, n_seg), ("det", "z", "xh", "y", "seg"))
    placed = (
        P("det", "seg", BANK),
        P(BANK, None, "seg"),
        P(BANK, None, None, "seg"),
        P(BANK),
        P((*BANK, "seg")),
        P(),
    )
    return jax.shard_map(
        shards, mesh=fine, in_specs=placed, out_specs=P((*BANK, "seg")), check_vma=False
    )
```

time: 52 us -> 46.2 us (0.89)
  waiting for transfers between devices: 13.2 us -> 6.57 us
  blocking collectives: 2 us -> 3.45 us
    all_to_all x2 -> x1, waiting for transfers between devices: 13.2 us -> 0.58 us  [shards(): lax.all_to_all(jnp.broadcast_to(piece[None, None], (n_chips, 1, LANES)),...]
    ppermute x1, waiting for transfers between devices: 0.01 us -> 5.98 us  [shards(): other = lax.ppermute(own, 'seg', [(0, 1), (1, 0)])]
    all_gather x1, blocking collectives: 2 us -> 3.45 us  [shards(): both = lax.all_gather(mine, 'det', axis=0, tiled=False)]
    sqrt x0 -> x1, local copies, waits for them, and re-layouts: none -> 0.57 us  [shards(): return jnp.sqrt(jnp.max(both[0] + both[1], axis=0))]
    broadcast_in_dim x2 -> x1, local copies, waits for them, and re-layouts: 1.27 us -> 0.72 us  [shards(): jnp.broadcast_to(piece[None, None], (n_chips, 1, LANES))]
    all_to_all x2 -> x1, starting transfers between devices: 24.9 us -> 24.3 us  [shards(): lax.all_to_all(jnp.broadcast_to(piece[None, None], (n_chips, 1, LANES)),...]
    unnamed x10 -> x9, local copies, waits for them, and re-layouts: 2.46 us -> 2.51 us
  transfers between devices with their start and end apart: 3 -> 2, of which waited for: 2 -> 2; matrix products, arithmetic and copies ran while one was open for 4% -> 3% of each run, Pallas kernels for 1% -> 2%
where the time goes in v1:
time: 46.2 us; the launch traced here: 45.9 us
  starting transfers between devices  27.5 us (60%)
  waiting for transfers between devices  6.57 us (14%)
  Pallas kernels  3.87 us (8%)
  local copies, waits for them, and re-layouts  3.81 us (8%)
  blocking collectives  3.45 us (7%)
  between operations  0.7 us (2%)
    all_to_all x1, starting transfers between devices, shards(): lax.all_to_all(jnp.broadcast_to(piece[None, None], (n_chips, 1, LANES)),...  24.3 us
    ppermute x1, waiting for transfers between devices, shards(): other = lax.ppermute(own, 'seg', [(0, 1), (1, 0)])  5.98 us
    all_gather x1, blocking collectives, shards(): both = lax.all_gather(mine, 'det', axis=0, tiled=False)  3.45 us
    pallas_call x1, Pallas kernels, shards(): pl.pallas_call(peaks_kernel, out_shape=jax.ShapeDtypeStruct((bins, width)...  3.11 us
    ppermute x1, starting transfers between devices, shards(): other = lax.ppermute(own, 'seg', [(0, 1), (1, 0)])  3.11 us
    unnamed x9, local copies, waits for them, and re-layouts  2.51 us
  transfers between devices with their start and end apart: 2, of which 2 were waited for; matrix products, arithmetic and copies ran while one was open for 3% of the time, Pallas kernels for 2%

profile of v1, /device:TPU:1, one launch (start us, length us, event | category | flops | bytes accessed | tf_op | source)
XLA Modules:
  0.0 45.9 jit_solution(17333777590047407196)
XLA Ops:
  0.0 0.0 copy-start.3
  0.0 0.0 copy-start
  0.0 0.7 %copy-done.3 = bf16[1,1,16]{2,1,0:T(2,128)(2,1)S(1)} copy-done((bf16[1,1,16]{2,1,0:T(2,128)(2,1)S(1)}, bf16[1,1,16]{2,1,0:T(2,128)(2,1)}, u32[]{:S(2)}) %copy-start.3) | copy-done | bytes 56
  0.7 0.7 %broadcast_in_dim.2 = f32[256,1,128]{2,1,0:T(1,128)} broadcast(f32[128]{0:T(128)S(1)} %pad_convert_fusion), dimensions={2} | broadcast | bytes 131584 | tf_op jit(solution)/shard_map/broadcast_in_dim | solution.py:109
  1.4 24.3 %all-to-all-start = ((f32[256,1,128]{2,1,0:T(1,128)}), f32[256,1,128]{2,1,0:T(1,128)S(1)}, u32[]{:S(2)}, u32[]{:S(2)}) async-start(f32[256,1,128]{2,1,0:T(1,128)} %broadcast_in_dim.2), calls=%async_computation | async-start | bytes 262144 | tf_op jit(solution)/shard_map/all_to_all | solution.py:108
  25.7 0.0 copy-done
  25.7 3.1 %collective-permute-start = (bf16[320,512]{1,0:T(8,128)(2,1)S(1)}, bf16[320,512]{1,0:T(8,128)(2,1)S(1)}, u32[]{:S(2)}, u32[]{:S(2)}) collective-permute-start(bf16[320,512]{1,0:T(8,128)(2,1)S(1)} %bitcast.13), channel_id=1, source_target_pairs={{0,1},{1,0},{2,3},{3,2},{4,5},{5,4},{6,7},{7,6},{8,9},{9,8},{10,11... | collective-permute-start | bytes 983048 | tf_op jit(solution)/shard_map/ppermute | solution.py:103
  28.9 1.2 %copy.10 = bf16[1,640,2,256]{3,1,2,0:T(8,128)(2,1)S(1)} copy(bf16[1,640,2,256]{3,2,1,0:T(2,128)(2,1)} %param.8) | data formatting | bytes 1310720 | tf_op args[2]
  30.7 6.0 %collective-permute-done.other_ref = bf16[320,512]{1,0:T(8,128)(2,1)S(1)} collective-permute-done((bf16[320,512]{1,0:T(8,128)(2,1)S(1)}, bf16[320,512]{1,0:T(8,128)(2,1)S(1)}, u32[]{:S(2)}, u32[]{:S(2)}) %collective-permute-start) | collective-permute-done | bytes 327712 | tf_op jit(solution)/shard_map/ppermute | solution.py:103
  36.7 0.8 %shard_map.64.filt_ref = bf16[512,512]{1,0:T(8,128)(2,1)S(1)} custom-call(s32[1]{0:T(128)S(6)} %copy.11.count_ref, bf16[320,512]{1,0:T(8,128)(2,1)S(1)} %bitcast.14, bf16[320,512]{1,0:T(8,128)(2,1)S(1)} %collective-permute-done.other_ref, bf16[2,640,256]{2,1,0:T(8,128)(2,1)S(1)} %bitcast.11), custom_call_target="tpu_custom_call" | custom-call | flops 335544320 | bytes 2097152 | tf_op jit(solution)/shard_map/pallas_call | solution.py:118
  37.4 0.6 %all-to-all-done = f32[256,1,128]{2,1,0:T(1,128)S(1)} async-done(((f32[256,1,128]{2,1,0:T(1,128)}), f32[256,1,128]{2,1,0:T(1,128)S(1)}, u32[]{:S(2)}, u32[]{:S(2)}) %all-to-all-start) | async-done | bytes 131104 | tf_op jit(solution)/shard_map/all_to_all | solution.py:108
  38.0 0.0 copy-start.1
  38.0 0.0 copy-start.2
  38.0 0.7 %copy-done.1 = s32[256]{0:T(256)S(1)} copy-done((s32[256]{0:T(256)S(1)}, s32[256]{0:T(256)}, u32[]{:S(2)}) %copy-start.1) | copy-done | bytes 1048
  38.7 0.0 copy-done.2
  38.7 3.1 %shard_map.65 = f32[32,256]{1,0:T(8,128)S(1)} custom-call(s32[2]{0:T(128)S(1)} %copy-done.2, f32[256,128]{1,0:T(8,128)S(1)} %bitcast.12, bf16[512,512]{1,0:T(8,128)(2,1)S(1)} %shard_map.64.filt_ref, s32[1,256]{1,0:T(1,128)S(1)} %bitcast.15), custom_call_target="tpu_custom_call" | custom-call | tf_op jit(solution)/shard_map/pallas_call | solution.py:128
  41.8 3.5 %all-gather = f32[64,256]{1,0:T(8,128)S(1)} all-gather(f32[32,256]{1,0:T(8,128)S(1)} %shard_map.65), channel_id=2, replica_groups=mesh['det'=2,'z'=16,'xh'=2,'y'=4,'seg'=2] {'det'}, dimensions={0}, use_global_device_ids=true | all-gather | bytes 98304 | tf_op jit(solution)/shard_map/all_gather | solution.py:139
  45.3 0.6 %sqrt.3 = f32[256]{0:T(256)} sqrt(f32[256]{0:T(256)S(1)} %fusion) | non-fusion elementwise | bytes 2048 | tf_op jit(solution)/shard_map/sqrt | solution.py:140
  (2 shorter events, 0.0 us)
Async XLA Ops:
  0.0 0.7 %copy-start.3 = (bf16[1,1,16]{2,1,0:T(2,128)(2,1)S(1)}, bf16[1,1,16]{2,1,0:T(2,128)(2,1)}, u32[]{:S(2)}) copy-start(bf16[1,1,16]{2,1,0:T(2,128)(2,1)} %param.6) | copy-start | bytes 100
  0.0 25.7 %copy-start = (bf16[1,512,320]{1,2,0:T(8,128)(2,1)S(1)}, bf16[1,512,320]{1,2,0:T(8,128)(2,1)}, u32[]{:S(2)}) copy-start(bf16[1,512,320]{1,2,0:T(8,128)(2,1)} %param.7) | copy-start | bytes 983044
  1.4 36.6 %all-to-all-start = ((f32[256,1,128]{2,1,0:T(1,128)}), f32[256,1,128]{2,1,0:T(1,128)S(1)}, u32[]{:S(2)}, u32[]{:S(2)}) async-start(f32[256,1,128]{2,1,0:T(1,128)} %broadcast_in_dim.2), calls=%async_computation | async-start | bytes 262144 | tf_op jit(solution)/shard_map/all_to_all | solution.py:108
  25.7 10.9 %collective-permute-start = (bf16[320,512]{1,0:T(8,128)(2,1)S(1)}, bf16[320,512]{1,0:T(8,128)(2,1)S(1)}, u32[]{:S(2)}, u32[]{:S(2)}) collective-permute-start(bf16[320,512]{1,0:T(8,128)(2,1)S(1)} %bitcast.13), channel_id=1, source_target_pairs={{0,1},{1,0},{2,3},{3,2},{4,5},{5,4},{6,7},{7,6},{8,9},{9,8},{10,11... | collective-permute-start | bytes 983048 | tf_op jit(solution)/shard_map/ppermute | solution.py:103
  38.0 0.7 %copy-start.1 = (s32[256]{0:T(256)S(1)}, s32[256]{0:T(256)}, u32[]{:S(2)}) copy-start(s32[256]{0:T(256)} %param.10) | copy-start | bytes 3076
  38.0 0.7 %copy-start.2 = (s32[2]{0:T(128)S(1)}, s32[2]{0:T(128)}, u32[]{:S(2)}) copy-start(s32[2]{0:T(128)} %slides_ref.1) | copy-start | bytes 28

commit v2 on v1

--- a/solution.py
+++ b/solution.py
@@ -7,17 +7,25 @@
 
 BIN = 128
 WMAX = 2
+LANES = 128
 FIRST_Z = 11
-LANES = 128
 CHIPS = ("xh", "y", "seg", "z")
 BANK = ("z", "xh", "y")
 
 
-def filters_kernel(count_ref, own_ref, other_ref, mix_ref, out_ref):
+def rows_kernel(count_ref, slides_ref, window_ref, counts_ref, limits_ref, turn_ref):
+    det = lax.axis_index("det")
+    bins = lax.axis_size("seg") * lax.axis_size("z")
+    counts_ref[...] = jnp.full(counts_ref.shape, count_ref[0], jnp.int32)
+    limits_ref[...] = jnp.where(det == 0, 0, window_ref[...])
+    turn_ref[...] = jnp.full(turn_ref.shape, lax.rem(bins - slides_ref[det], bins), jnp.int32)
+
+
+def filters_kernel(counts_ref, own_ref, other_ref, mix_ref, out_ref):
     seg = lax.axis_index("seg")
     half = own_ref.shape[0]
     width = mix_ref.shape[2]
-    count = count_ref[0]
+    count = counts_ref[...]
     for quad in range(2):
         total = None
         for place, filters in ((seg, own_ref), (1 - seg, other_ref)):
@@ -32,7 +40,7 @@
         out_ref[:, quad * width : (quad + 1) * width] = total.astype(jnp.bfloat16)
 
 
-def peaks_kernel(slides_ref, pieces_ref, filt_ref, limits_ref, out_ref, hankel, power):
+def peaks_kernel(turn_ref, pieces_ref, filt_ref, limits_ref, out_ref, hankel, power):
     bins, width = out_ref.shape
     n_z = bins // 2
     fine = pieces_ref.shape[0] // bins
@@ -61,29 +69,33 @@
         )
 
     here = turned(0)
-    for c in range(bins + spans - 1):
-        after = turned(c + 1) if c + 1 < bins else jnp.zeros((BIN, LANES), jnp.float32)
-        tile = jnp.where(early, here, after).astype(jnp.bfloat16)
-        here = after
-        for span in range(spans):
-            if 0 <= c - span < bins:
-                hankel[pl.ds((c - span) * BIN, BIN), span * LANES : (span + 1) * LANES] = tile
+    made = 0
     for first in range(0, bins, group):
+        while made < first + group + spans - 1:
+            after = turned(made + 1) if made + 1 < bins else jnp.zeros((BIN, LANES), jnp.float32)
+            tile = jnp.where(early, here, after).astype(jnp.bfloat16)
+            here = after
+            for span in range(spans):
+                if 0 <= made - span < bins:
+                    hankel[pl.ds((made - span) * BIN, BIN), span * LANES : (span + 1) * LANES] = tile
+            made += 1
         snr = jnp.dot(
             hankel[pl.ds(first * BIN, group * BIN), :], filt, preferred_element_type=jnp.float32
         )
         real, imag = snr[:, :width], snr[:, width:]
         squared = (real * real + imag * imag).reshape(group, BIN, width)
-        peak = jnp.max(squared, axis=1)
-        power[pl.ds(first, group), :] = peak
+        power[pl.ds(first, group), :] = jnp.max(squared, axis=1)
 
-    det = lax.axis_index("det")
-    limits = jnp.where(det == 0, 0, limits_ref[...])
-    shifted = pltpu.roll(power[...], lax.rem(bins - slides_ref[det], bins), 0)
+    limits = limits_ref[...]
+    turn = turn_ref[...]
+    shifted = power[...]
+    for bit in range((bins - 1).bit_length()):
+        moved = pltpu.roll(shifted, 1 << bit, 0)
+        shifted = jnp.where(((turn >> bit) & 1) == 1, moved, shifted)
     best = shifted
     for offset in range(1, WMAX + 1):
-        for turn in (offset, bins - offset):
-            moved = pltpu.roll(shifted, turn, 0)
+        for step in (offset, bins - offset):
+            moved = pltpu.roll(shifted, step, 0)
             best = jnp.maximum(best, jnp.where(limits >= offset, moved, 0.0))
     out_ref[...] = best
 
@@ -91,10 +103,11 @@
 def shards(strain, basis_filters, template_mix, basis_counts, window_bins, time_slides):
     taps = basis_filters.shape[1]
     width = template_mix.shape[3]
+    n_z = lax.axis_size("z")
     n_chips = 1
     for axis in CHIPS:
         n_chips *= lax.axis_size(axis)
-    bins = lax.axis_size("seg") * lax.axis_size("z")
+    bins = lax.axis_size("seg") * n_z
 
     vmem = pl.BlockSpec(memory_space=pltpu.VMEM)
     smem = pl.BlockSpec(memory_space=pltpu.SMEM)
@@ -102,9 +115,8 @@
     own = jnp.transpose(basis_filters[0])
     other = lax.ppermute(own, "seg", [(0, 1), (1, 0)])
 
+    order = [c - c % n_z + (c + FIRST_Z) % n_z for c in range(n_chips)]
     piece = jnp.pad(strain[0, 0].astype(jnp.float32), (0, LANES - strain.shape[2]))
-    n_z = lax.axis_size("z")
-    order = [c - c % n_z + (c + FIRST_Z) % n_z for c in range(n_chips)]
     pieces = lax.all_to_all(
         jnp.broadcast_to(piece[None, None], (n_chips, 1, LANES)),
         CHIPS,
@@ -112,30 +124,37 @@
         0,
         axis_index_groups=[order],
         tiled=True,
-    ).reshape(n_chips, LANES)
+    )
+    pieces = pieces.reshape(n_chips, LANES)
 
+    counts, limits, turn = pl.pallas_call(
+        rows_kernel,
+        out_shape=(pltpu.VMEM((1, width), jnp.int32),) * 3,
+        in_specs=[smem, smem, vmem],
+        out_specs=(vmem, vmem, vmem),
+    )(basis_counts, time_slides, window_bins.reshape(1, width))
     mix = jnp.transpose(template_mix[0], (1, 0, 2))
     filt = pl.pallas_call(
         filters_kernel,
         out_shape=jax.ShapeDtypeStruct((taps, 2 * width), jnp.bfloat16),
-        in_specs=[smem, vmem, vmem, vmem],
+        in_specs=[vmem, vmem, vmem, vmem],
         out_specs=vmem,
         compiler_params=pltpu.CompilerParams(vmem_limit_bytes=24 << 20),
         cost_estimate=pl.CostEstimate(
-            flops=1 * 4 * taps * width * mix.shape[1], bytes_accessed=2 << 20, transcendentals=0
+            flops=4 * taps * width * mix.shape[1], bytes_accessed=2 << 20, transcendentals=0
         ),
-    )(basis_counts, own, other, mix)
+    )(counts, own, other, mix)
     mine = pl.pallas_call(
         peaks_kernel,
         out_shape=jax.ShapeDtypeStruct((bins, width), jnp.float32),
-        in_specs=[smem, vmem, vmem, vmem],
+        in_specs=[vmem, vmem, vmem, vmem],
         out_specs=vmem,
         scratch_shapes=[
             pltpu.VMEM((bins * BIN, taps), jnp.bfloat16),
             pltpu.VMEM((bins, width), jnp.float32),
         ],
         compiler_params=pltpu.CompilerParams(vmem_limit_bytes=32 << 20),
-    )(time_slides, pieces, filt, window_bins.reshape(1, width))
+    )(turn, pieces, filt, limits)
     both = lax.all_gather(mine, "det", axis=0, tiled=False)
     return jnp.sqrt(jnp.max(both[0] + both[1], axis=0))
 

time: 46.2 us -> 44.9 us (0.972)
  local copies, waits for them, and re-layouts: 3.81 us -> 3.12 us
  waiting for transfers between devices: 6.57 us -> 6.08 us
    ppermute x1, waiting for transfers between devices: 5.98 us -> 5.25 us  [shards(): other = lax.ppermute(own, 'seg', [(0, 1), (1, 0)])]
    pallas_call x0 -> x1, Pallas kernels: none -> 0.71 us  [shards(): pl.pallas_call(rows_kernel, out_shape=(pltpu.VMEM((1, width), jnp.int32),...]
    unnamed x9 -> x5, local copies, waits for them, and re-layouts: 2.51 us -> 1.83 us
    pallas_call x1, Pallas kernels: 3.11 us -> 2.57 us  [shards(): pl.pallas_call(peaks_kernel, out_shape=jax.ShapeDtypeStruct((bins, width)...]
  transfers between devices with their start and end apart: 2 -> 2, of which waited for: 2 -> 2; matrix products, arithmetic and copies ran while one was open for 3% -> 3% of each run, Pallas kernels for 2% -> 3%
where the time goes in v2:
time: 44.9 us; the launch traced here: 44.7 us
  starting transfers between devices  27.5 us (61%)
  waiting for transfers between devices  6.08 us (14%)
  Pallas kernels  4.04 us (9%)
  blocking collectives  3.25 us (7%)
  local copies, waits for them, and re-layouts  3.12 us (7%)
  between operations  0.7 us (2%)
    all_to_all x1, starting transfers between devices, shards(): lax.all_to_all(jnp.broadcast_to(piece[None, None], (n_chips, 1, LANES)),...  24.3 us
    ppermute x1, waiting for transfers between devices, shards(): other = lax.ppermute(own, 'seg', [(0, 1), (1, 0)])  5.25 us
    all_gather x1, blocking collectives, shards(): both = lax.all_gather(mine, 'det', axis=0, tiled=False)  3.25 us
    ppermute x1, starting transfers between devices, shards(): other = lax.ppermute(own, 'seg', [(0, 1), (1, 0)])  3.11 us
    pallas_call x1, Pallas kernels, shards(): pl.pallas_call(peaks_kernel, out_shape=jax.ShapeDtypeStruct((bins, width)...  2.57 us
    unnamed x5, local copies, waits for them, and re-layouts  1.83 us
  transfers between devices with their start and end apart: 2, of which 2 were waited for; matrix products, arithmetic and copies ran while one was open for 3% of the time, Pallas kernels for 3%

profile of v2, /device:TPU:1, one launch (start us, length us, event | category | flops | bytes accessed | tf_op | source)
XLA Modules:
  0.0 44.7 jit_solution(7555874522868115308)
XLA Ops:
  0.0 0.0 copy-start.1
  0.0 0.0 copy-start
  0.0 0.7 %copy-done.1 = bf16[1,1,16]{2,1,0:T(2,128)(2,1)S(1)} copy-done((bf16[1,1,16]{2,1,0:T(2,128)(2,1)S(1)}, bf16[1,1,16]{2,1,0:T(2,128)(2,1)}, u32[]{:S(2)}) %copy-start.1) | copy-done | bytes 56
  0.7 0.7 %broadcast_in_dim.2 = f32[256,1,128]{2,1,0:T(1,128)} broadcast(f32[128]{0:T(128)S(1)} %pad_convert_fusion), dimensions={2} | broadcast | bytes 131584 | tf_op jit(solution)/shard_map/broadcast_in_dim | solution.py:121
  1.4 24.3 %all-to-all-start = ((f32[256,1,128]{2,1,0:T(1,128)}), f32[256,1,128]{2,1,0:T(1,128)S(1)}, u32[]{:S(2)}, u32[]{:S(2)}) async-start(f32[256,1,128]{2,1,0:T(1,128)} %broadcast_in_dim.2), calls=%async_computation | async-start | bytes 262144 | tf_op jit(solution)/shard_map/all_to_all | solution.py:120
  25.7 0.0 copy-done
  25.7 3.1 %collective-permute-start = (bf16[320,512]{1,0:T(8,128)(2,1)S(1)}, bf16[320,512]{1,0:T(8,128)(2,1)S(1)}, u32[]{:S(2)}, u32[]{:S(2)}) collective-permute-start(bf16[320,512]{1,0:T(8,128)(2,1)S(1)} %bitcast.13), channel_id=1, source_target_pairs={{0,1},{1,0},{2,3},{3,2},{4,5},{5,4},{6,7},{7,6},{8,9},{9,8},{10,11... | collective-permute-start | bytes 983048 | tf_op jit(solution)/shard_map/ppermute | solution.py:116
  29.5 1.2 %copy.10 = bf16[1,640,2,256]{3,1,2,0:T(8,128)(2,1)S(1)} copy(bf16[1,640,2,256]{3,2,1,0:T(2,128)(2,1)} %param.8) | data formatting | bytes 1310720 | tf_op args[2]
  30.7 0.7 %shard_map.64 = (s32[1,256]{1,0:T(1,128)S(1)}, s32[1,256]{1,0:T(1,128)S(1)}, s32[1,256]{1,0:T(1,128)S(1)}) custom-call(s32[1]{0:T(128)S(6)} %copy.11.count_ref, s32[2]{0:T(128)} %slides_ref.1, s32[1,256]{1,0:T(1,128)} %bitcast.15), custom_call_target="tpu_custom_call" | custom-call | tf_op jit(solution)/shard_map/pallas_call | solution.py:130
  31.4 5.2 %collective-permute-done.other_ref = bf16[320,512]{1,0:T(8,128)(2,1)S(1)} collective-permute-done((bf16[320,512]{1,0:T(8,128)(2,1)S(1)}, bf16[320,512]{1,0:T(8,128)(2,1)S(1)}, u32[]{:S(2)}, u32[]{:S(2)}) %collective-permute-start) | collective-permute-done | bytes 327712 | tf_op jit(solution)/shard_map/ppermute | solution.py:116
  36.7 0.8 %shard_map.65.filt_ref = bf16[512,512]{1,0:T(8,128)(2,1)S(1)} custom-call(s32[1,256]{1,0:T(1,128)S(1)} %get-tuple-element.9.counts_ref, bf16[320,512]{1,0:T(8,128)(2,1)S(1)} %bitcast.14, bf16[320,512]{1,0:T(8,128)(2,1)S(1)} %collective-permute-done.other_ref, bf16[2,640,256]{2,1,0:T(8,128)(2,1)S(1)} %bitcast.11), custom_call_target="tpu_custom_call" | custom-call | flops 335544320 | bytes 2097152 | tf_op jit(solution)/shard_map/pallas_call | solution.py:137
  37.4 0.8 %all-to-all-done = f32[256,1,128]{2,1,0:T(1,128)S(1)} async-done(((f32[256,1,128]{2,1,0:T(1,128)}), f32[256,1,128]{2,1,0:T(1,128)S(1)}, u32[]{:S(2)}, u32[]{:S(2)}) %all-to-all-start) | async-done | bytes 131104 | tf_op jit(solution)/shard_map/all_to_all | solution.py:120
  38.3 2.6 %shard_map.66 = f32[32,256]{1,0:T(8,128)S(1)} custom-call(s32[1,256]{1,0:T(1,128)S(1)} %get-tuple-element.8.turn_ref, f32[256,128]{1,0:T(8,128)S(1)} %bitcast.12, bf16[512,512]{1,0:T(8,128)(2,1)S(1)} %shard_map.65.filt_ref, s32[1,256]{1,0:T(1,128)S(1)} %get-tuple-element.10.limits_ref), custom_call_target="tpu_custom_call" | custom-call | tf_op jit(solution)/shard_map/pallas_call | solution.py:147
  40.8 3.3 %all-gather = f32[64,256]{1,0:T(8,128)S(1)} all-gather(f32[32,256]{1,0:T(8,128)S(1)} %shard_map.66), channel_id=2, replica_groups=mesh['det'=2,'z'=16,'xh'=2,'y'=4,'seg'=2] {'det'}, dimensions={0}, use_global_device_ids=true | all-gather | bytes 98304 | tf_op jit(solution)/shard_map/all_gather | solution.py:158
  44.1 0.6 %sqrt.3 = f32[256]{0:T(256)} sqrt(f32[256]{0:T(256)S(1)} %fusion) | non-fusion elementwise | bytes 2048 | tf_op jit(solution)/shard_map/sqrt | solution.py:159
  (2 shorter events, 0.0 us)
Async XLA Ops:
  0.0 0.7 %copy-start.1 = (bf16[1,1,16]{2,1,0:T(2,128)(2,1)S(1)}, bf16[1,1,16]{2,1,0:T(2,128)(2,1)}, u32[]{:S(2)}) copy-start(bf16[1,1,16]{2,1,0:T(2,128)(2,1)} %param.6) | copy-start | bytes 100
  0.0 25.7 %copy-start = (bf16[1,512,320]{1,2,0:T(8,128)(2,1)S(1)}, bf16[1,512,320]{1,2,0:T(8,128)(2,1)}, u32[]{:S(2)}) copy-start(bf16[1,512,320]{1,2,0:T(8,128)(2,1)} %param.7) | copy-start | bytes 983044
  1.4 36.9 %all-to-all-start = ((f32[256,1,128]{2,1,0:T(1,128)}), f32[256,1,128]{2,1,0:T(1,128)S(1)}, u32[]{:S(2)}, u32[]{:S(2)}) async-start(f32[256,1,128]{2,1,0:T(1,128)} %broadcast_in_dim.2), calls=%async_computation | async-start | bytes 262144 | tf_op jit(solution)/shard_map/all_to_all | solution.py:120
  25.7 10.9 %collective-permute-start = (bf16[320,512]{1,0:T(8,128)(2,1)S(1)}, bf16[320,512]{1,0:T(8,128)(2,1)S(1)}, u32[]{:S(2)}, u32[]{:S(2)}) collective-permute-start(bf16[320,512]{1,0:T(8,128)(2,1)S(1)} %bitcast.13), channel_id=1, source_target_pairs={{0,1},{1,0},{2,3},{3,2},{4,5},{5,4},{6,7},{7,6},{8,9},{9,8},{10,11... | collective-permute-start | bytes 983048 | tf_op jit(solution)/shard_map/ppermute | solution.py:116

commit v3 on v2

--- a/solution.py
+++ b/solution.py
@@ -113,7 +113,11 @@
     smem = pl.BlockSpec(memory_space=pltpu.SMEM)
 
     own = jnp.transpose(basis_filters[0])
-    other = lax.ppermute(own, "seg", [(0, 1), (1, 0)])
+    part = own.shape[0] // lax.axis_size("det")
+    fetched = lax.ppermute(
+        lax.dynamic_slice_in_dim(own, lax.axis_index("det") * part, part, 0), "seg", [(0, 1), (1, 0)]
+    )
+    other = lax.all_gather(fetched, "det", axis=0, tiled=True)
 
     order = [c - c % n_z + (c + FIRST_Z) % n_z for c in range(n_chips)]
     piece = jnp.pad(strain[0, 0].astype(jnp.float32), (0, LANES - strain.shape[2]))
@@ -141,7 +145,7 @@
         out_specs=vmem,
         compiler_params=pltpu.CompilerParams(vmem_limit_bytes=24 << 20),
         cost_estimate=pl.CostEstimate(
-            flops=4 * taps * width * mix.shape[1], bytes_accessed=2 << 20, transcendentals=0
+            flops=1 * taps * width * mix.shape[1], bytes_accessed=2 << 20, transcendentals=0
         ),
     )(counts, own, other, mix)
     mine = pl.pallas_call(

time: 44.9 us -> 45 us (level)
  waiting for transfers between devices: 6.08 us -> 2.5 us
  blocking collectives: 3.25 us -> 6.81 us
    ppermute x1, waiting for transfers between devices: 5.25 us -> 1.56 us  [shards(): lax.ppermute(lax.dynamic_slice_in_dim(own, lax.axis_index('det') * part,...]
    all_gather x0 -> x1, blocking collectives: none -> 3.55 us  [shards(): other = lax.all_gather(fetched, 'det', axis=0, tiled=True)]
where the time goes in v3:
time: 45 us; the launch traced here: 44.7 us
  starting transfers between devices  27.5 us (61%)
  blocking collectives  6.81 us (15%)
  Pallas kernels  4.03 us (9%)
  local copies, waits for them, and re-layouts  3.14 us (7%)
  waiting for transfers between devices  2.5 us (6%)
  between operations  0.72 us (2%)
    all_to_all x1, starting transfers between devices, shards(): lax.all_to_all(jnp.broadcast_to(piece[None, None], (n_chips, 1, LANES)),...  24.3 us
    all_gather x1, blocking collectives, shards(): other = lax.all_gather(fetched, 'det', axis=0, tiled=True)  3.55 us
    all_gather x1, blocking collectives, shards(): both = lax.all_gather(mine, 'det', axis=0, tiled=False)  3.26 us
    ppermute x1, starting transfers between devices, shards(): lax.ppermute(lax.dynamic_slice_in_dim(own, lax.axis_index('det') * part,...  3.11 us
    pallas_call x1, Pallas kernels, shards(): pl.pallas_call(peaks_kernel, out_shape=jax.ShapeDtypeStruct((bins, width)...  2.57 us
    unnamed x5, local copies, waits for them, and re-layouts  1.83 us
    ppermute x1, waiting for transfers between devices, shards(): lax.ppermute(lax.dynamic_slice_in_dim(own, lax.axis_index('det') * part,...  1.56 us
    all_to_all x1, waiting for transfers between devices, shards(): lax.all_to_all(jnp.broadcast_to(piece[None, None], (n_chips, 1, LANES)),...  0.94 us
  transfers between devices with their start and end apart: 2, of which 2 were waited for; matrix products, arithmetic and copies ran while one was open for 3% of the time, Pallas kernels for 3%

profile of v3, /device:TPU:1, one launch (start us, length us, event | category | flops | bytes accessed | tf_op | source)
XLA Modules:
  0.0 44.7 jit_solution(9330535474456977957)
XLA Ops:
  0.0 0.0 copy-start.1
  0.0 0.0 copy-start
  0.0 0.7 %copy-done.1 = bf16[1,1,16]{2,1,0:T(2,128)(2,1)S(1)} copy-done((bf16[1,1,16]{2,1,0:T(2,128)(2,1)S(1)}, bf16[1,1,16]{2,1,0:T(2,128)(2,1)}, u32[]{:S(2)}) %copy-start.1) | copy-done | bytes 56
  0.7 0.7 %broadcast_in_dim.2 = f32[256,1,128]{2,1,0:T(1,128)} broadcast(f32[128]{0:T(128)S(1)} %pad_convert_fusion), dimensions={2} | broadcast | bytes 131584 | tf_op jit(solution)/shard_map/broadcast_in_dim | solution.py:125
  1.4 24.3 %all-to-all-start = ((f32[256,1,128]{2,1,0:T(1,128)}), f32[256,1,128]{2,1,0:T(1,128)S(1)}, u32[]{:S(2)}, u32[]{:S(2)}) async-start(f32[256,1,128]{2,1,0:T(1,128)} %broadcast_in_dim.2), calls=%async_computation | async-start | bytes 262144 | tf_op jit(solution)/shard_map/all_to_all | solution.py:124
  25.7 0.0 copy-done
  25.8 3.1 %collective-permute-start = (bf16[160,512]{1,0:T(8,128)(2,1)S(1)}, bf16[160,512]{1,0:T(8,128)(2,1)S(1)}, u32[]{:S(2)}, u32[]{:S(2)}) collective-permute-start(bf16[160,512]{1,0:T(8,128)(2,1)S(1)} %dynamic-slice_bitcast_fusion), channel_id=1, source_target_pairs={{0,1},{1,0},{2,3},{3,2},{4,5},{5,4},{6,7},{7,6},{8,9},{9,8},{10,11... | collective-permute-start | bytes 491528 | tf_op jit(solution)/shard_map/ppermute | solution.py:117
  29.5 1.2 %copy.10 = bf16[1,640,2,256]{3,1,2,0:T(8,128)(2,1)S(1)} copy(bf16[1,640,2,256]{3,2,1,0:T(2,128)(2,1)} %param.8) | data formatting | bytes 1310720 | tf_op args[2]
  30.7 0.7 %shard_map.64 = (s32[1,256]{1,0:T(1,128)S(1)}, s32[1,256]{1,0:T(1,128)S(1)}, s32[1,256]{1,0:T(1,128)S(1)}) custom-call(s32[1]{0:T(128)S(6)} %copy.11.count_ref, s32[2]{0:T(128)} %slides_ref.1, s32[1,256]{1,0:T(1,128)} %bitcast.18), custom_call_target="tpu_custom_call" | custom-call | tf_op jit(solution)/shard_map/pallas_call | solution.py:134
  31.4 1.6 %collective-permute-done = bf16[160,512]{1,0:T(8,128)(2,1)S(1)} collective-permute-done((bf16[160,512]{1,0:T(8,128)(2,1)S(1)}, bf16[160,512]{1,0:T(8,128)(2,1)S(1)}, u32[]{:S(2)}, u32[]{:S(2)}) %collective-permute-start) | collective-permute-done | bytes 163872 | tf_op jit(solution)/shard_map/ppermute | solution.py:117
  33.0 3.5 %all_gather.9.other_ref = bf16[320,512]{1,0:T(8,128)(2,1)S(1)} all-gather(bf16[160,512]{1,0:T(8,128)(2,1)S(1)} %collective-permute-done), channel_id=1, replica_groups=mesh['det'=2,'z'=16,'xh'=2,'y'=4,'seg'=2] {'det'}, dimensions={0}, use_global_device_ids=true | all-gather | bytes 491520 | tf_op jit(solution)/shard_map/all_gather | solution.py:120
  36.5 0.8 %shard_map.65.filt_ref = bf16[512,512]{1,0:T(8,128)(2,1)S(1)} custom-call(s32[1,256]{1,0:T(1,128)S(1)} %get-tuple-element.9.counts_ref, bf16[320,512]{1,0:T(8,128)(2,1)S(1)} %bitcast.16, bf16[320,512]{1,0:T(8,128)(2,1)S(1)} %all_gather.9.other_ref, bf16[2,640,256]{2,1,0:T(8,128)(2,1)S(1)} %bitcast.15), custom_call_target="tpu_custom_call" | custom-call | flops 83886080 | bytes 2097152 | tf_op jit(solution)/shard_map/pallas_call | solution.py:141
  37.3 0.9 %all-to-all-done = f32[256,1,128]{2,1,0:T(1,128)S(1)} async-done(((f32[256,1,128]{2,1,0:T(1,128)}), f32[256,1,128]{2,1,0:T(1,128)S(1)}, u32[]{:S(2)}, u32[]{:S(2)}) %all-to-all-start) | async-done | bytes 131104 | tf_op jit(solution)/shard_map/all_to_all | solution.py:124
  38.3 2.6 %shard_map.66 = f32[32,256]{1,0:T(8,128)S(1)} custom-call(s32[1,256]{1,0:T(1,128)S(1)} %get-tuple-element.8.turn_ref, f32[256,128]{1,0:T(8,128)S(1)} %bitcast.17, bf16[512,512]{1,0:T(8,128)(2,1)S(1)} %shard_map.65.filt_ref, s32[1,256]{1,0:T(1,128)S(1)} %get-tuple-element.10.limits_ref), custom_call_target="tpu_custom_call" | custom-call | tf_op jit(solution)/shard_map/pallas_call | solution.py:151
  40.8 3.3 %all-gather = f32[64,256]{1,0:T(8,128)S(1)} all-gather(f32[32,256]{1,0:T(8,128)S(1)} %shard_map.66), channel_id=2, replica_groups=mesh['det'=2,'z'=16,'xh'=2,'y'=4,'seg'=2] {'det'}, dimensions={0}, use_global_device_ids=true | all-gather | bytes 98304 | tf_op jit(solution)/shard_map/all_gather | solution.py:162
  44.1 0.6 %sqrt.3 = f32[256]{0:T(256)} sqrt(f32[256]{0:T(256)S(1)} %fusion) | non-fusion elementwise | bytes 2048 | tf_op jit(solution)/shard_map/sqrt | solution.py:163
  (3 shorter events, 0.0 us)
Async XLA Ops:
  0.0 0.7 %copy-start.1 = (bf16[1,1,16]{2,1,0:T(2,128)(2,1)S(1)}, bf16[1,1,16]{2,1,0:T(2,128)(2,1)}, u32[]{:S(2)}) copy-start(bf16[1,1,16]{2,1,0:T(2,128)(2,1)} %param.6) | copy-start | bytes 100
  0.0 25.7 %copy-start = (bf16[1,512,320]{1,2,0:T(8,128)(2,1)S(1)}, bf16[1,512,320]{1,2,0:T(8,128)(2,1)}, u32[]{:S(2)}) copy-start(bf16[1,512,320]{1,2,0:T(8,128)(2,1)} %param.7) | copy-start | bytes 983044
  1.4 36.9 %all-to-all-start = ((f32[256,1,128]{2,1,0:T(1,128)}), f32[256,1,128]{2,1,0:T(1,128)S(1)}, u32[]{:S(2)}, u32[]{:S(2)}) async-start(f32[256,1,128]{2,1,0:T(1,128)} %broadcast_in_dim.2), calls=%async_computation | async-start | bytes 262144 | tf_op jit(solution)/shard_map/all_to_all | solution.py:124
  25.8 7.2 %collective-permute-start = (bf16[160,512]{1,0:T(8,128)(2,1)S(1)}, bf16[160,512]{1,0:T(8,128)(2,1)S(1)}, u32[]{:S(2)}, u32[]{:S(2)}) collective-permute-start(bf16[160,512]{1,0:T(8,128)(2,1)S(1)} %dynamic-slice_bitcast_fusion), channel_id=1, source_target_pairs={{0,1},{1,0},{2,3},{3,2},{4,5},{5,4},{6,7},{7,6},{8,9},{9,8},{10,11... | collective-permute-start | bytes 491528 | tf_op jit(solution)/shard_map/ppermute | solution.py:117
